TPU v7x, 256 devices: a whole 4x4x8 slice. The times are simulated.
256 devices in a mesh: dp: 16 (over x, y), ctx: 16 (over z, core).
Axes of the slice: x: 4, y: 4, z: 8, core: 2. Of those that a mesh axis runs over, the one named last changes fastest.
Arguments:
- q_nope: bfloat16 [64, 128, 128], P('dp', 'ctx'), may hold values from -6 to 6
- q_rope: bfloat16 [64, 128, 64], P('dp', 'ctx'), may hold values from -8 to 8
- w_uk: bfloat16 [128, 128, 512], P('ctx'), may hold values from -0.5 to 0.5
- w_uv: bfloat16 [128, 512, 128], P('ctx'), may hold values from -6 to 6
- w_out: bfloat16 [16384, 7168], P('ctx', 'dp'), may hold values from -0.046875 to 0.046875
- latent_cache: bfloat16 [64, 32768, 576], P('dp', 'ctx'), may hold values from -8 to 8
- lengths: int32 [64], P('dp'), may hold values from 1 to 32768, as said below
Outputs:
- layer_out: bfloat16 [64, 7168], P('ctx', 'dp')
Inputs may be any that keep to these rules, and one draw needn't show every extreme that they name: `lengths`: cached positions of each sequence; some sequence fills all 32768.
All inputs are finite; a program needn't handle non-finite values.
Results may differ from a plain program's by a relative error of at most 0.024.
Values may be sent and summed in bfloat16 or wider, within the bound.
A program may use at most 128 MiB of HBM per device.

v0:
```python
import math

import jax
import jax.numpy as jnp
from jax import lax
from jax.sharding import PartitionSpec as P


def finish(numerator, denominator, w_uv):
    latent_out = (numerator / denominator[..., None]).astype(jnp.bfloat16)
    head_out = jnp.einsum(
        "shl,hlv->shv", latent_out, w_uv, preferred_element_type=jnp.float32
    ).astype(jnp.bfloat16)
    return head_out.reshape(head_out.shape[0], head_out.shape[1] * head_out.shape[2])


def per_device(q_nope, q_rope, w_uk, w_uv, w_out, latent_cache, lengths):
    seq_local = q_nope.shape[0]
    latent_width = w_uk.shape[2]
    ctx_local = latent_cache.shape[1]
    softmax_scale = 1.0 / math.sqrt(q_nope.shape[2] + q_rope.shape[2])
    q_latent = jnp.einsum("shn,hnl->shl", q_nope, w_uk, preferred_element_type=jnp.float32).astype(
        jnp.bfloat16
    )
    query_local = jnp.concatenate([q_latent, q_rope], axis=2)
    queries = lax.all_gather(query_local, "ctx", axis=1, tiled=True)
    heads_all = queries.shape[1]
    block_rows = min(512, ctx_local)
    count_blocks = ctx_local // block_rows
    first_position = lax.axis_index("ctx") * ctx_local

    def visit(number, carry):
        highest, running_sum, running_out = carry
        offset = number * block_rows
        cache_block = lax.dynamic_slice_in_dim(latent_cache, offset, block_rows, 1)
        scores = (
            jnp.einsum("shc,skc->shk", queries, cache_block, preferred_element_type=jnp.float32)
            * softmax_scale
        )
        position = first_position + offset + jnp.arange(block_rows, dtype=jnp.int32)
        is_live = (position[None, :] < lengths[:, None])[:, None, :]
        masked = jnp.where(is_live, scores, -1e30)
        newest = jnp.maximum(highest, jnp.max(masked, axis=2))
        exponent = jnp.where(is_live, jnp.exp(masked - newest[:, :, None]), 0.0)
        rescale = jnp.exp(highest - newest)
        running_sum = running_sum * rescale + jnp.sum(exponent, axis=2)
        update = jnp.einsum(
            "shk,skl->shl",
            exponent.astype(jnp.bfloat16),
            cache_block[:, :, :latent_width],
            preferred_element_type=jnp.float32,
        )
        running_out = running_out * rescale[..., None] + update
        return (newest, running_sum, running_out)

    start_carry = (
        jnp.full((seq_local, heads_all), -1e30, jnp.float32),
        jnp.zeros((seq_local, heads_all), jnp.float32),
        jnp.zeros((seq_local, heads_all, latent_width), jnp.float32),
    )
    highest, running_sum, running_out = lax.fori_loop(0, count_blocks, visit, start_carry)
    peak_all = lax.all_to_all(highest[None], "ctx", split_axis=2, concat_axis=0, tiled=True)
    sums_all = lax.all_to_all(running_sum[None], "ctx", split_axis=2, concat_axis=0, tiled=True)
    outs_all = lax.all_to_all(running_out[None], "ctx", split_axis=2, concat_axis=0, tiled=True)
    peak_value = jnp.max(peak_all, axis=0)
    weight = jnp.exp(peak_all - peak_value[None])
    numerator = jnp.sum(weight[..., None] * outs_all, axis=0)
    denominator = jnp.sum(weight * sums_all, axis=0)
    heads_local = finish(numerator, denominator, w_uv)
    partial_terms = jnp.dot(
        lax.all_gather(heads_local, "dp", axis=0, tiled=True),
        w_out,
        preferred_element_type=jnp.float32,
    )
    return lax.psum_scatter(partial_terms, "ctx", scatter_dimension=0, tiled=True).astype(
        jnp.bfloat16
    )


def solution(mesh):
    in_specs = (
        P("dp", "ctx", None),
        P("dp", "ctx", None),
        P("ctx", None, None),
        P("ctx", None, None),
        P("ctx", "dp"),
        P("dp", "ctx", None),
        P("dp"),
    )
    out_specs = P("ctx", "dp")
    return jax.shard_map(
        per_device, mesh=mesh, in_specs=in_specs, out_specs=out_specs, check_vma=False
    )
```

profile of v0, /device:TPU:1, one launch (start us, length us, event | category | flops | bytes accessed | tf_op | source)
XLA Modules:
  0.0 178.0 jit_solution(7656141930192381813)
XLA Ops:
  0.0 0.0 copy-start
  0.0 0.8 copy.21
  0.8 0.4 copy-done
  1.2 0.9 fusion.26
  2.2 23.1 %all_gather.6 = bf16[4,128,576]{2,0,1:T(4,128)(2,1)S(1)} all-gather(bf16[4,8,576]{2,0,1:T(4,128)(2,1)S(1)} %pad_maximum_fusion), channel_id=1, replica_groups=mesh['dp'=16,'ctx'=16] {'ctx'}, dimensions={1}, use_global_device_ids=true | all-gather | bytes 626688 | tf_op jit(solution)/shard_map/all_gather | solution.py:26
  25.3 1.3 copy.22
  26.6 0.0 copy-start.1
  26.6 26.3 %while.18 = (s32[]{:T(128)}, f32[4,128]{1,0:T(4,128)S(1)}, f32[4,128]{1,0:T(4,128)S(1)}, f32[4,128,512]{2,1,0:T(8,128)S(1)}, s32[]{:T(128)}, /*index=5*/s32[4]{0...) while((s32[]{:T(128)}, f32[4,128]{1,0:T(4,128)S(1)}, ...), condition=%wide.region_3.4_spmd.clone, body=%wide.region_0.3_spmd.clone.sunk | while | flops 573576192 | bytes 10334423 | solution.py:61
  26.6 0.7 broadcast_compare_fusion.2
  27.4 2.7 %fusion.51 = (f32[4,128]{1,0:T(4,128)S(1)}, f32[4,128,512]{1,2,0:T(8,128)S(1)}) fusion(bf16[4,128,576]{1,2,0:T(8,128)(2,1)} %get-tuple-element.310, bf16[4,2048,576]{1,2,0:T(8,128)(2,1)} %get-tuple-element.309, s32[]{:T(128)S(6)} %select_n.43, pred[4,512]{1,0:T(4,128)(4,1)S(1)} %broadcast_compare_fusion.2), kind=kOutput, calls=%fused_computation.41.clone.1 | convolution fusion | flops 302775808 | bytes 4001796 | tf_op jit(solution)/shard_map/while/body/eval_jaxpr/shc,skc->shk/dot_general | solution.py:37
  30.2 0.4 fusion.52
  30.5 2.7 %fusion.54 = f32[4,128,512]{2,1,0:T(8,128)S(1)} fusion(bf16[4,2048,576]{1,2,0:T(8,128)(2,1)} %get-tuple-element.309, s32[]{:T(128)S(6)} %select_n.43, f32[4,128,512]{2,1,0:T(8,128)S(1)} %get-tuple-element.294, f32[4,128,512]{1,2,0:T(8,128)S(1)} %get-tuple-element.276, f32[4,128]{1,0:T(4,128)S(1)} %get-tuple-element.278, ...), kind=kOutput, calls=%fused_computation.4.clone.1 | convolution fusion | flops 270008320 | bytes 5249029 | tf_op jit(solution)/shard_map/while/body/eval_jaxpr/shk,skl->shl/dot_general | solution.py:47
  33.2 0.7 broadcast_compare_fusion.2
  34.0 2.7 %fusion.51 = (f32[4,128]{1,0:T(4,128)S(1)}, f32[4,128,512]{1,2,0:T(8,128)S(1)}) fusion(bf16[4,128,576]{1,2,0:T(8,128)(2,1)} %get-tuple-element.310, bf16[4,2048,576]{1,2,0:T(8,128)(2,1)} %get-tuple-element.309, s32[]{:T(128)S(6)} %select_n.43, pred[4,512]{1,0:T(4,128)(4,1)S(1)} %broadcast_compare_fusion.2), kind=kOutput, calls=%fused_computation.41.clone.1 | convolution fusion | flops 302775808 | bytes 4001796 | tf_op jit(solution)/shard_map/while/body/eval_jaxpr/shc,skc->shk/dot_general | solution.py:37
  36.7 0.4 fusion.52
  37.1 2.7 %fusion.54 = f32[4,128,512]{2,1,0:T(8,128)S(1)} fusion(bf16[4,2048,576]{1,2,0:T(8,128)(2,1)} %get-tuple-element.309, s32[]{:T(128)S(6)} %select_n.43, f32[4,128,512]{2,1,0:T(8,128)S(1)} %get-tuple-element.294, f32[4,128,512]{1,2,0:T(8,128)S(1)} %get-tuple-element.276, f32[4,128]{1,0:T(4,128)S(1)} %get-tuple-element.278, ...), kind=kOutput, calls=%fused_computation.4.clone.1 | convolution fusion | flops 270008320 | bytes 5249029 | tf_op jit(solution)/shard_map/while/body/eval_jaxpr/shk,skl->shl/dot_general | solution.py:47
  39.8 0.7 broadcast_compare_fusion.2
  40.5 2.7 %fusion.51 = (f32[4,128]{1,0:T(4,128)S(1)}, f32[4,128,512]{1,2,0:T(8,128)S(1)}) fusion(bf16[4,128,576]{1,2,0:T(8,128)(2,1)} %get-tuple-element.310, bf16[4,2048,576]{1,2,0:T(8,128)(2,1)} %get-tuple-element.309, s32[]{:T(128)S(6)} %select_n.43, pred[4,512]{1,0:T(4,128)(4,1)S(1)} %broadcast_compare_fusion.2), kind=kOutput, calls=%fused_computation.41.clone.1 | convolution fusion | flops 302775808 | bytes 4001796 | tf_op jit(solution)/shard_map/while/body/eval_jaxpr/shc,skc->shk/dot_general | solution.py:37
  43.3 0.4 fusion.52
  43.7 2.7 %fusion.54 = f32[4,128,512]{2,1,0:T(8,128)S(1)} fusion(bf16[4,2048,576]{1,2,0:T(8,128)(2,1)} %get-tuple-element.309, s32[]{:T(128)S(6)} %select_n.43, f32[4,128,512]{2,1,0:T(8,128)S(1)} %get-tuple-element.294, f32[4,128,512]{1,2,0:T(8,128)S(1)} %get-tuple-element.276, f32[4,128]{1,0:T(4,128)S(1)} %get-tuple-element.278, ...), kind=kOutput, calls=%fused_computation.4.clone.1 | convolution fusion | flops 270008320 | bytes 5249029 | tf_op jit(solution)/shard_map/while/body/eval_jaxpr/shk,skl->shl/dot_general | solution.py:47
  46.4 0.7 broadcast_compare_fusion.2
  47.1 2.7 %fusion.51 = (f32[4,128]{1,0:T(4,128)S(1)}, f32[4,128,512]{1,2,0:T(8,128)S(1)}) fusion(bf16[4,128,576]{1,2,0:T(8,128)(2,1)} %get-tuple-element.310, bf16[4,2048,576]{1,2,0:T(8,128)(2,1)} %get-tuple-element.309, s32[]{:T(128)S(6)} %select_n.43, pred[4,512]{1,0:T(4,128)(4,1)S(1)} %broadcast_compare_fusion.2), kind=kOutput, calls=%fused_computation.41.clone.1 | convolution fusion | flops 302775808 | bytes 4001796 | tf_op jit(solution)/shard_map/while/body/eval_jaxpr/shc,skc->shk/dot_general | solution.py:37
  49.9 0.4 fusion.52
  50.3 2.7 %fusion.54 = f32[4,128,512]{2,1,0:T(8,128)S(1)} fusion(bf16[4,2048,576]{1,2,0:T(8,128)(2,1)} %get-tuple-element.309, s32[]{:T(128)S(6)} %select_n.43, f32[4,128,512]{2,1,0:T(8,128)S(1)} %get-tuple-element.294, f32[4,128,512]{1,2,0:T(8,128)S(1)} %get-tuple-element.276, f32[4,128]{1,0:T(4,128)S(1)} %get-tuple-element.278, ...), kind=kOutput, calls=%fused_computation.4.clone.1 | convolution fusion | flops 270008320 | bytes 5249029 | tf_op jit(solution)/shard_map/while/body/eval_jaxpr/shk,skl->shl/dot_general | solution.py:47
  52.9 0.7 copy.23
  53.7 3.8 %all-to-all-start = ((f32[1,4,128]{1,0,2:T(1,128)}), f32[1,4,128]{1,0,2:T(1,128)S(1)}, u32[]{:S(2)}, u32[]{:S(2)}) async-start(f32[1,4,128]{1,0,2:T(1,128)} %bitcast.1), calls=%async_computation | async-start | bytes 131072 | tf_op jit(solution)/shard_map/all_to_all | solution.py:62
  57.5 0.7 copy.27
  58.2 7.1 %all-to-all-done = f32[1,4,128]{1,0,2:T(1,128)S(1)} async-done(((f32[1,4,128]{1,0,2:T(1,128)}), f32[1,4,128]{1,0,2:T(1,128)S(1)}, u32[]{:S(2)}, u32[]{:S(2)}) %all-to-all-start) | async-done | bytes 2080 | tf_op jit(solution)/shard_map/all_to_all | solution.py:62
  65.3 3.4 %all-to-all-start.2 = ((f32[1,4,128]{1,0,2:T(1,128)}), f32[1,4,128]{1,0,2:T(1,128)S(1)}, u32[]{:S(2)}, u32[]{:S(2)}) async-start(f32[1,4,128]{1,0,2:T(1,128)} %bitcast.9), calls=%async_computation.2 | async-start | bytes 131072 | tf_op jit(solution)/shard_map/all_to_all | solution.py:63
  68.7 1.7 copy.40
  70.4 6.2 %all-to-all-done.2 = f32[1,4,128]{1,0,2:T(1,128)S(1)} async-done(((f32[1,4,128]{1,0,2:T(1,128)}), f32[1,4,128]{1,0,2:T(1,128)S(1)}, u32[]{:S(2)}, u32[]{:S(2)}) %all-to-all-start.2) | async-done | bytes 2080 | tf_op jit(solution)/shard_map/all_to_all | solution.py:63
  76.6 3.6 %all-to-all-start.1 = ((f32[1,4,128,512]{3,1,0,2:T(4,128)}), f32[1,4,128,512]{3,1,0,2:T(4,128)S(1)}, u32[]{:S(2)}, u32[]{:S(2)}) async-start(f32[1,4,128,512]{3,1,0,2:T(4,128)} %bitcast.41), calls=%async_computation.1 | async-start | bytes 2097152 | tf_op jit(solution)/shard_map/all_to_all | solution.py:64
  80.2 0.0 copy-done.1
  80.2 0.6 dynamic-slice
  81.4 0.2 copy.32
  81.6 0.2 copy.33
  81.8 26.3 %all-to-all-done.1 = f32[1,4,128,512]{3,1,0,2:T(4,128)S(1)} async-done(((f32[1,4,128,512]{3,1,0,2:T(4,128)}), f32[1,4,128,512]{3,1,0,2:T(4,128)S(1)}, u32[]{:S(2)}, u32[]{:S(2)}) %all-to-all-start.1) | async-done | bytes 1048608 | tf_op jit(solution)/shard_map/all_to_all | solution.py:64
  108.1 0.3 fusion.28
  108.5 0.1 divide_convert_fusion
  108.5 1.5 fusion.27
  110.0 18.7 %all-gather = bf16[16,4,1024]{2,1,0:T(4,128)(2,1)S(1)} all-gather(bf16[1,4,1024]{2,1,0:T(4,128)(2,1)S(1)} %fusion.27), channel_id=1, replica_groups=mesh['dp'=16,'ctx'=16] {'dp'}, dimensions={0}, use_global_device_ids=true | all-gather | bytes 139264 | tf_op jit(solution)/shard_map/all_gather | solution.py:71
  128.8 1.6 fusion.35
  130.4 47.0 %all-reduce = bf16[64,448]{1,0:T(8,128)(2,1)S(1)} all-reduce(f32[64,448]{1,0:T(8,128)S(1)} %fusion.35), channel_id=2, replica_groups=mesh['dp'=16,'ctx'=16] {'ctx'}, use_global_device_ids=true, to_apply=%region_7.8.clone | all-reduce | flops 28672 | bytes 172032
  177.4 0.6 dynamic-slice_convert_fusion
  (23 shorter events, 0.2 us)
Async XLA Ops:
  0.0 1.2 copy-start
  26.6 53.5 %copy-start.1 = (u32[256]{0:T(256)S(1)}, u32[256]{0:T(256)}, u32[]{:S(2)}) copy-start(u32[256]{0:T(256)} %constant.76) | copy-start | bytes 3076
  53.7 11.6 %all-to-all-start = ((f32[1,4,128]{1,0,2:T(1,128)}), f32[1,4,128]{1,0,2:T(1,128)S(1)}, u32[]{:S(2)}, u32[]{:S(2)}) async-start(f32[1,4,128]{1,0,2:T(1,128)} %bitcast.1), calls=%async_computation | async-start | bytes 131072 | tf_op jit(solution)/shard_map/all_to_all | solution.py:62
  65.3 11.3 %all-to-all-start.2 = ((f32[1,4,128]{1,0,2:T(1,128)}), f32[1,4,128]{1,0,2:T(1,128)S(1)}, u32[]{:S(2)}, u32[]{:S(2)}) async-start(f32[1,4,128]{1,0,2:T(1,128)} %bitcast.9), calls=%async_computation.2 | async-start | bytes 131072 | tf_op jit(solution)/shard_map/all_to_all | solution.py:63
  76.6 31.6 %all-to-all-start.1 = ((f32[1,4,128,512]{3,1,0,2:T(4,128)}), f32[1,4,128,512]{3,1,0,2:T(4,128)S(1)}, u32[]{:S(2)}, u32[]{:S(2)}) async-start(f32[1,4,128,512]{3,1,0,2:T(4,128)} %bitcast.41), calls=%async_computation.1 | async-start | bytes 2097152 | tf_op jit(solution)/shard_map/all_to_all | solution.py:64
where the time goes:
time: 180 us; the launch traced here: 178 us
  blocking collectives  88.9 us (49%)
  waiting for transfers between devices  39.6 us (22%)
  matrix products  25.6 us (14%)
  starting transfers between devices  10.8 us (6%)
  local copies, waits for them, and re-layouts  7.24 us (4%)
  other arithmetic  4.94 us (3%)
    unnamed x1, blocking collectives  47 us
    all_to_all x1, waiting for transfers between devices, per_device(): lax.all_to_all(running_out[None], 'ctx', split_axis=2, concat_axis=0, til...  26.3 us
    all_gather x1, blocking collectives, per_device(): queries = lax.all_gather(query_local, 'ctx', axis=1, tiled=True)  23.1 us
    all_gather x1, blocking collectives, per_device(): lax.all_gather(heads_local, 'dp', axis=0, tiled=True)  18.7 us
    dot_general x4, matrix products, visit(): jnp.einsum('shc,skc->shk', queries, cache_block, preferred_element_type=j...  11 us
    dot_general x4, matrix products, visit(): jnp.einsum('shk,skl->shl', exponent.astype(jnp.bfloat16), cache_block[:,...  10.6 us
    all_to_all x1, waiting for transfers between devices, per_device(): lax.all_to_all(highest[None], 'ctx', split_axis=2, concat_axis=0, tiled=T...  7.08 us
    all_to_all x1, waiting for transfers between devices, per_device(): lax.all_to_all(running_sum[None], 'ctx', split_axis=2, concat_axis=0, til...  6.17 us
  transfers between devices with their start and end apart: 3, of which 3 were waited for; matrix products, arithmetic and copies ran while one was open for 2% of the time, Pallas kernels for 0%

commit v1 on v0

v1 whole, which is shorter than its diff:
```python
import functools
import math

import jax
import jax.numpy as jnp
from jax import lax
from jax.experimental import pallas as pl
from jax.experimental.pallas import tpu as pltpu
from jax.sharding import PartitionSpec as P

MESH = pl.DeviceIdType.MESH
F32 = jnp.float32
BF16 = jnp.bfloat16
FLOOR = -(2.0**90)


def far_first(n):
    return sorted(range(1, n), key=lambda d: -min(d, n - d))


def near_first(n):
    return sorted(range(1, n), key=lambda d: min(d, n - d))


def columns(shape, values):
    lane = lax.broadcasted_iota(jnp.int32, shape, 1)
    out = jnp.zeros(shape, F32)
    for at, value in enumerate(values):
        out = jnp.where(lane == at, value, out)
    return out


def spread(rows, heads):
    count, width = rows.shape
    wide = jnp.concatenate([rows.astype(F32)] * heads, axis=1)
    row_head = lax.rem(lax.broadcasted_iota(jnp.int32, wide.shape, 0), heads)
    col_head = lax.div(lax.broadcasted_iota(jnp.int32, wide.shape, 1), width)
    return jnp.where(row_head == col_head, wide, 0.0).astype(BF16)


def dot_nt(a, b):
    return lax.dot_general(a, b, (((1,), (1,)), ((), ())), preferred_element_type=F32)


def kernel(
    nz,
    ndp,
    scale2,
    lengths,
    qn_hbm,
    qr_hbm,
    wuk_hbm,
    wuv_hbm,
    wout_hbm,
    cache_hbm,
    out_ref,
    qn,
    qr,
    wuk,
    wuv,
    wout,
    cache,
    q0,
    q1,
    qfull,
    scores,
    probs,
    acc_mine,
    acc_other,
    st_mine,
    st_other,
    o_send,
    o_recv,
    heads_buf,
    heads_f32,
    sums_f32,
    sums_send,
    sums_recv,
    out_f32,
    load_sem,
    cache_sem,
    q_ss,
    q_rs,
    f_ss,
    f_rs,
    p_ss,
    p_rs,
    o_ss,
    o_rs,
    h_ss,
    h_rs,
    t_ss,
    t_rs,
):
    nctx = 2 * nz
    i = lax.axis_index("dp")
    c = lax.axis_index("ctx")
    z = lax.div(c, 2)
    k = lax.rem(c, 2)
    other = 1 - k
    seqs, width, span = cache.shape
    lat = wuk.shape[1]
    rope = width - lat
    heads = wuk.shape[0] // qn.shape[1]

    def z_at(d):
        return lax.rem(z + d, nz)

    def z_peer(d):
        return (i, z_at(d) * 2 + k)

    partner = (i, z * 2 + other)

    def ctx_at(d):
        return lax.rem(c + d, nctx)

    def dp_at(d):
        return lax.rem(i + d, ndp)

    loads = [
        pltpu.make_async_copy(src, dst, load_sem.at[n])
        for n, (src, dst) in enumerate(
            ((qn_hbm, qn), (wuk_hbm, wuk), (qr_hbm, qr), (wuv_hbm, wuv), (wout_hbm, wout))
        )
    ]
    for load in loads[:3]:
        load.start()

    barrier = pltpu.get_barrier_semaphore()
    for d in far_first(nctx):
        pl.semaphore_signal(barrier, inc=1, device_id=(i, ctx_at(d)), device_id_type=MESH)
    for d in far_first(ndp):
        pl.semaphore_signal(barrier, inc=1, device_id=(dp_at(d), c), device_id_type=MESH)

    cache_loads = [
        pltpu.make_async_copy(cache_hbm.at[s], cache.at[s], cache_sem.at[s]) for s in range(seqs)
    ]
    for load in cache_loads:
        load.start()
    for load in loads[3:]:
        load.start()

    for load in loads[:3]:
        load.wait()
    q_lat = jnp.dot(spread(qn[...], heads), wuk[...], preferred_element_type=F32)
    half = q_lat.shape[0] // 2
    q0[k, z, :, :lat] = q_lat[:half].astype(BF16)
    q1[k, z] = q_lat[half:].astype(BF16)
    rope_rows = qr[...].astype(F32)
    q0[k, z, :, lat:] = jnp.concatenate([rope_rows[:half], rope_rows[half:]], axis=1).astype(BF16)

    pl.semaphore_wait(barrier, nctx + ndp - 2)

    q_bufs = (q0, q1)

    def remote(src, dst, ss, rs, device):
        return pltpu.make_async_remote_copy(
            src_ref=src, dst_ref=dst, send_sem=ss, recv_sem=rs, device_id=device, device_id_type=MESH
        )

    sent = []

    def send(*args):
        copy = remote(*args)
        copy.start()
        sent.append(copy)

    for a, buf in enumerate(q_bufs):
        own = buf.at[k, z]
        for d in far_first(nz):
            send(own, own, q_ss.at[a, d], q_rs.at[a, d], z_peer(d))
        send(own, own, f_ss.at[a, 0], f_rs.at[a, 0], partner)

    def forward(a):
        buf = q_bufs[a]
        for d in near_first(nz):
            slot = buf.at[k, z_at(nz - d)]
            remote(slot, slot, q_ss.at[a, d], q_rs.at[a, d], z_peer(d)).wait_recv()
            send(slot, slot, f_ss.at[a, d], f_rs.at[a, d], partner)

    def gathered(a):
        buf = q_bufs[a]
        for d in [0] + near_first(nz):
            slot = buf.at[other, z_at(nz - d) if d else z]
            remote(slot, slot, f_ss.at[a, d], f_rs.at[a, d], partner).wait_recv()

    block = min(512, span)

    def rows_of(buf, u, start, stop):
        rows = buf[:, :, :, start:stop].astype(F32)
        rows = rows.reshape(nctx, 2, heads, stop - start)
        return rows[:, u].reshape(nctx * heads, stop - start)

    def attend(a):
        stats = []
        for u in range(2):
            s = 2 * a + u
            cache_loads[s].wait()
            qfull[:, :lat] = rows_of(q_bufs[a], u, 0, lat).astype(BF16)
            ropes = rows_of(q0, u, lat, lat + 2 * rope)
            qfull[:, lat:] = ropes[:, a * rope : (a + 1) * rope].astype(BF16)
            top = jnp.full((nctx * heads, 128), -1e30, F32)
            live = lengths[s] - c * span
            for b in range(span // block):
                part = jnp.dot(
                    qfull[...],
                    cache[s, :, b * block : (b + 1) * block],
                    preferred_element_type=F32,
                )
                position = b * block + lax.broadcasted_iota(jnp.int32, part.shape, 1)
                part = jnp.where(position < live, part, -1e30)
                scores[:, b * block : (b + 1) * block] = part
                for e in range(block // 128):
                    top = jnp.maximum(top, part[:, e * 128 : (e + 1) * 128])
            m2 = jnp.maximum(jnp.max(top, axis=1, keepdims=True) * scale2, FLOOR)
            total = jnp.zeros((nctx * heads, 128), F32)
            for b in range(span // block):
                part = jnp.exp2(scores[:, b * block : (b + 1) * block] * scale2 - m2)
                probs[:, b * block : (b + 1) * block] = part.astype(BF16)
                for e in range(block // 128):
                    total = total + part[:, e * 128 : (e + 1) * 128]
            stats += [m2, jnp.sum(total, axis=1, keepdims=True)]
            acc = dot_nt(probs[...], cache[s, :lat, :]).astype(BF16)
            mid = nz * heads
            acc_mine[a, 0, u] = acc[:mid]
            acc_mine[a, 1, u] = acc[mid:]
        table = columns((nctx * heads, 128), stats)
        st_mine[a, 0] = table[: nz * heads]
        st_mine[a, 1] = table[nz * heads :]
        send(acc_mine.at[a, other], acc_other.at[a], p_ss.at[a, 0], p_rs.at[a, 0], partner)
        send(st_mine.at[a, other], st_other.at[a], p_ss.at[a, 1], p_rs.at[a, 1], partner)

    def exchange(a):
        remote(
            acc_mine.at[a, other], acc_other.at[a], p_ss.at[a, 0], p_rs.at[a, 0], partner
        ).wait_recv()
        remote(
            st_mine.at[a, other], st_other.at[a], p_ss.at[a, 1], p_rs.at[a, 1], partner
        ).wait_recv()
        mine, theirs = st_mine[a, k], st_other[a]
        data, stats = [], []
        for u in range(2):
            m_a, l_a = mine[:, 2 * u : 2 * u + 1], mine[:, 2 * u + 1 : 2 * u + 2]
            m_b, l_b = theirs[:, 2 * u : 2 * u + 1], theirs[:, 2 * u + 1 : 2 * u + 2]
            m = jnp.maximum(m_a, m_b)
            m_hi = m.astype(BF16).astype(F32)
            m_lo = (m - m_hi).astype(BF16).astype(F32)
            m = m_hi + m_lo
            w_a, w_b = jnp.exp2(m_a - m), jnp.exp2(m_b - m)
            l = w_a * l_a + w_b * l_b
            l_hi = l.astype(BF16).astype(F32)
            l_lo = l - l_hi
            joined = w_a * acc_mine[a, k, u].astype(F32) + w_b * acc_other[a, u].astype(F32)
            data.append(joined.reshape(nz, 1, heads, lat))
            table = columns((nz * heads, 128), (m_hi, m_lo, l_hi, l_lo))
            stats.append(table.reshape(nz, 1, heads, 128))
        data = jnp.concatenate(data, axis=1).reshape(nz, 2 * heads, lat)
        stats = jnp.concatenate(stats, axis=1).reshape(nz, 2 * heads, 128)
        o_send[a, :, :, :lat] = data.astype(BF16)
        o_send[a, :, :, lat:] = stats.astype(BF16)
        for d in far_first(nz):
            send(o_send.at[a, z_at(d)], o_recv.at[a, z], o_ss.at[a, d], o_rs.at[a, d], z_peer(d))
        o_recv[a, z] = o_send[a, z]

    def finish(a):
        for d in near_first(nz):
            came = z_at(nz - d)
            remote(
                o_send.at[a, came], o_recv.at[a, came], o_ss.at[a, d], o_rs.at[a, d], z_peer(d)
            ).wait_recv()
        tops, sums = [], []
        for n in range(nz):
            table = o_recv[a, n, :, lat:].astype(F32)
            tops.append(table[:, 0:1] + table[:, 1:2])
            sums.append(table[:, 2:3] + table[:, 3:4])
        top = functools.reduce(jnp.maximum, tops)
        numerator = jnp.zeros((2 * heads, lat), F32)
        denominator = jnp.zeros((2 * heads, 1), F32)
        for n in range(nz):
            w = jnp.exp2(tops[n] - top)
            denominator = denominator + w * sums[n]
            numerator = numerator + w * o_recv[a, n, :, :lat].astype(F32)
        return numerator / denominator

    forward(0)
    gathered(0)
    attend(0)
    forward(1)
    exchange(0)
    gathered(1)
    attend(1)
    exchange(1)
    latents = jnp.concatenate([finish(0), finish(1)], axis=0).astype(BF16)

    loads[3].wait()
    head_out = jnp.dot(spread(latents, heads), wuv[...], preferred_element_type=F32)
    heads_buf[i] = head_out.astype(BF16)
    for d in far_first(ndp):
        own = heads_buf.at[i]
        send(own, own, h_ss.at[d], h_rs.at[d], (dp_at(d), c))
    loads[4].wait()
    for d in near_first(ndp):
        slot = heads_buf.at[dp_at(ndp - d)]
        remote(slot, slot, h_ss.at[d], h_rs.at[d], (dp_at(d), c)).wait_recv()
    heads_f32[...] = heads_buf[...].astype(F32).reshape(heads_f32.shape)
    rows = ndp * seqs
    merged = jnp.concatenate(
        [heads_f32[pl.ds(h, rows, stride=heads), :] for h in range(heads)], axis=1
    ).astype(BF16)
    terms = dot_nt(merged, wout[...])
    cols = terms.shape[1]
    pieces = -(-cols // 128)
    for n in range(pieces):
        piece = terms[:, n * 128 : min(cols, (n + 1) * 128)]
        if piece.shape[1] < 128:
            piece = jnp.concatenate(
                [piece, jnp.zeros((rows, 128 - piece.shape[1]), F32)], axis=1
            )
        sums_f32[pl.ds(n, rows, stride=pieces), :] = piece
    sums_send[...] = sums_f32[...].astype(BF16).reshape(sums_send.shape)
    for d in far_first(nctx):
        send(
            sums_send.at[ctx_at(d)], sums_recv.at[c], t_ss.at[d], t_rs.at[d], (i, ctx_at(d))
        )
    sums_recv[c] = sums_send[c]
    for d in near_first(nctx):
        came = ctx_at(nctx - d)
        remote(
            sums_send.at[came], sums_recv.at[came], t_ss.at[d], t_rs.at[d], (i, ctx_at(d))
        ).wait_recv()
    out_f32[...] = jnp.sum(sums_recv[...].astype(F32), axis=0)
    out_rows = out_ref.shape[0]
    for n in range(pieces):
        end = min(cols, (n + 1) * 128)
        piece = out_f32[pl.ds(n, out_rows, stride=pieces), :]
        out_ref[:, n * 128 : end] = piece[:, : end - n * 128].astype(BF16)
    for copy in sent:
        copy.wait_send()


def per_device(nz, ndp, q_nope, q_rope, w_uk, w_uv, w_out, latent_cache, lengths):
    seqs, heads, dn = q_nope.shape
    rope = q_rope.shape[2]
    lat = w_uk.shape[2]
    span = latent_cache.shape[1]
    dv = w_uv.shape[2]
    cols = w_out.shape[1]
    nctx = 2 * nz
    every = nctx * heads
    pieces = -(-cols // 128)
    out_rows = ndp * seqs // nctx
    scale2 = math.log2(math.e) / math.sqrt(dn + rope)
    vmem, dma = pltpu.VMEM, pltpu.SemaphoreType.DMA
    hbm = pl.BlockSpec(memory_space=pltpu.HBM)
    return pl.pallas_call(
        functools.partial(kernel, nz, ndp, scale2),
        out_shape=jax.ShapeDtypeStruct((out_rows, cols), BF16),
        in_specs=[pl.BlockSpec(memory_space=pltpu.SMEM)] + [hbm] * 6,
        out_specs=pl.BlockSpec(memory_space=vmem),
        scratch_shapes=[
            vmem((seqs * heads, dn), BF16),
            vmem((seqs * heads, rope), BF16),
            vmem((heads * dn, lat), BF16),
            vmem((heads * lat, dv), BF16),
            vmem((cols, heads * dv), BF16),
            vmem((seqs, lat + rope, span), BF16),
            vmem((2, nz, 2 * heads, lat + 2 * rope), BF16),
            vmem((2, nz, 2 * heads, lat), BF16),
            vmem((every, lat + rope), BF16),
            vmem((every, span), F32),
            vmem((every, span), BF16),
            vmem((2, 2, 2, nz * heads, lat), BF16),
            vmem((2, 2, nz * heads, lat), BF16),
            vmem((2, 2, nz * heads, 128), F32),
            vmem((2, nz * heads, 128), F32),
            vmem((2, nz, 2 * heads, lat + 128), BF16),
            vmem((2, nz, 2 * heads, lat + 128), BF16),
            vmem((ndp, seqs * heads, dv), BF16),
            vmem((ndp * seqs * heads, dv), F32),
            vmem((ndp * seqs * pieces, 128), F32),
            vmem((nctx, out_rows * pieces, 128), BF16),
            vmem((nctx, out_rows * pieces, 128), BF16),
            vmem((out_rows * pieces, 128), F32),
            dma((5,)),
            dma((seqs,)),
            dma((2, nz)),
            dma((2, nz)),
            dma((2, nz)),
            dma((2, nz)),
            dma((2, 2)),
            dma((2, 2)),
            dma((2, nz)),
            dma((2, nz)),
            dma((ndp,)),
            dma((ndp,)),
            dma((nctx,)),
            dma((nctx,)),
        ],
        compiler_params=pltpu.CompilerParams(
            collective_id=0, has_side_effects=True, vmem_limit_bytes=60 << 20
        ),
        name="mla_decode",
    )(
        lengths,
        q_nope.reshape(seqs * heads, dn),
        q_rope.reshape(seqs * heads, rope),
        w_uk.reshape(heads * dn, lat),
        w_uv.reshape(heads * lat, dv),
        w_out.T,
        jnp.swapaxes(latent_cache, 1, 2),
    )


def solution(mesh):
    in_specs = (
        P("dp", "ctx", None),
        P("dp", "ctx", None),
        P("ctx", None, None),
        P("ctx", None, None),
        P("ctx", "dp"),
        P("dp", "ctx", None),
        P("dp"),
    )
    out_specs = P("ctx", "dp")
    return jax.shard_map(
        functools.partial(per_device, mesh.shape["ctx"] // 2, mesh.shape["dp"]),
        mesh=mesh,
        in_specs=in_specs,
        out_specs=out_specs,
        check_vma=False,
    )
```

time: 180 us -> 47.3 us (0.26)
  blocking collectives: 88.9 us -> 0 us
  Pallas kernels: 0 us -> 45.8 us
  waiting for transfers between devices: 39.6 us -> 0 us
  matrix products: 25.6 us -> 0 us
  starting transfers between devices: 10.8 us -> 0 us
  local copies, waits for them, and re-layouts: 7.24 us -> 1.28 us
  other arithmetic: 4.94 us -> 0 us
    unnamed x1 -> x0, blocking collectives: 47 us -> none
    pallas_call x0 -> x1, Pallas kernels: none -> 45.8 us  [per_device(): pl.pallas_call(functools.partial(kernel, nz, ndp, scale2), out_shape=jax....]
    all_gather x2 -> x0, blocking collectives: 41.8 us -> none  [the longest x1 23.1 us: per_device(): queries = lax.all_gather(query_local, 'ctx', axis=1, tiled=True)]
    all_to_all x3 -> x0, waiting for transfers between devices: 39.6 us -> none  [the longest x1 26.3 us: per_device(): lax.all_to_all(running_out[None], 'ctx', split_axis=2, concat_axis=0, til...]
    dot_general x11 -> x0, matrix products: 25.6 us -> none  [the longest x4 11 us: visit(): jnp.einsum('shc,skc->shk', queries, cache_block, preferred_element_type=j...]
    all_to_all x3 -> x0, starting transfers between devices: 10.8 us -> none  [the longest x1 3.8 us: per_device(): lax.all_to_all(highest[None], 'ctx', split_axis=2, concat_axis=0, tiled=T...]
    while x7 -> x0, local copies, waits for them, and re-layouts: 3.13 us -> none  [the longest x3 3.12 us: per_device(): lax.fori_loop(0, count_blocks, visit, start_carry)]
    lt x4 -> x0, other arithmetic: 2.93 us -> none  [visit(): is_live = (position[None, :] < lengths[:, None])[:, None, :]]
  transfers between devices with their start and end apart: 3 -> 0, of which waited for: 3 -> 0; matrix products, arithmetic and copies ran while one was open for 2% -> 0% of each run, Pallas kernels for 0% -> 0%
where the time goes in v1:
time: 47.3 us; the launch traced here: 47.1 us
  Pallas kernels  45.8 us (97%)
  local copies, waits for them, and re-layouts  1.28 us (3%)
    pallas_call x1, Pallas kernels, per_device(): pl.pallas_call(functools.partial(kernel, nz, ndp, scale2), out_shape=jax....  45.8 us
    unnamed x1, local copies, waits for them, and re-layouts  1.28 us

profile of v1, /device:TPU:1, one launch (start us, length us, event | category | flops | bytes accessed | tf_op | source)
XLA Modules:
  0.0 47.1 jit_solution(7454121262931620780)
XLA Ops:
  0.0 45.8 %mla_decode.1 = bf16[4,448]{1,0:T(4,128)(2,1)} custom-call(s32[4]{0:T(128)} %lengths.1, bf16[32,128]{1,0:T(8,128)(2,1)} %bitcast.10, bf16[32,64]{1,0:T(8,128)(2,1)} %bitcast.11, bf16[1024,512]{1,0:T(8,128)(2,1)} %bitcast.7, bf16[4096,128]{1,0:T(8,128)(2,1)} %bitcast.8, bf16[448,1024]{1,0:T(8,128)(2,1)} %bitcast.9, bf16[4,576,2048]{2,1,0:T(8,128)(2,1)} %bitcast.6), custom_call_target="tpu_custom_call" | custom-call | tf_op jit(solution)/shard_map/mla_decode/pallas_call | solution.py:355
  45.8 1.3 %copy.9 = bf16[4,448]{1,0:T(4,128)(2,1)} copy(bf16[4,448]{1,0:T(4,128)(2,1)} %mla_decode.1) | data formatting | bytes 7168

commit v2 on v1

v2 whole, which is shorter than its diff:
```python
import functools
import math

import jax
import jax.numpy as jnp
from jax import lax
from jax.experimental import pallas as pl
from jax.experimental.pallas import tpu as pltpu
from jax.sharding import PartitionSpec as P

MESH = pl.DeviceIdType.MESH
F32 = jnp.float32
BF16 = jnp.bfloat16
FLOOR = -(2.0**90)


def far_first(n, size):
    step = lax.div(n + 1, 2)
    return size // 2 + jnp.where(lax.rem(n, 2) == 1, -step, step)


def near_first(n, size):
    return far_first(size - 2 - n, size)


AWAY = (0, 1, 7, 2, 6, 3, 5, 4)


def loop(count, body):
    lax.fori_loop(0, count, lambda n, carry: (body(n), carry)[1], 0)


def columns(shape, values):
    lane = lax.broadcasted_iota(jnp.int32, shape, 1)
    out = jnp.zeros(shape, F32)
    for at, value in values:
        out = jnp.where(lane == at, value, out)
    return out


def spread(rows, heads):
    count, width = rows.shape
    wide = jnp.concatenate([rows.astype(F32)] * heads, axis=1)
    row_head = lax.rem(lax.broadcasted_iota(jnp.int32, wide.shape, 0), heads)
    col_head = lax.div(lax.broadcasted_iota(jnp.int32, wide.shape, 1), width)
    return jnp.where(row_head == col_head, wide, 0.0).astype(BF16)


def dot_nt(a, b):
    return lax.dot_general(a, b, (((1,), (1,)), ((), ())), preferred_element_type=F32)


def remote(src, dst, ss, rs, device):
    return pltpu.make_async_remote_copy(
        src_ref=src, dst_ref=dst, send_sem=ss, recv_sem=rs, device_id=device, device_id_type=MESH
    )


def kernel(
    nz,
    ndp,
    scale2,
    len_hbm,
    qn_hbm,
    qr_hbm,
    wuk_hbm,
    wuv_hbm,
    wout_hbm,
    cache_hbm,
    out_ref,
    lengths,
    qn,
    qr,
    wuk,
    wuv,
    wout,
    cache,
    values,
    q_buf,
    r_buf,
    qfull,
    scores,
    probs,
    st_mine,
    st_other,
    acc_mine,
    acc_other,
    zs_send,
    zs_recv,
    o_send,
    o_recv,
    latents,
    heads_buf,
    heads_f32,
    sums_f32,
    sums_send,
    sums_recv,
    out_f32,
    load_sem,
    cache_sem,
    q_ss,
    q_rs,
    f_ss,
    f_rs,
    p_ss,
    p_rs,
    s_ss,
    s_rs,
    o_ss,
    o_rs,
    h_ss,
    h_rs,
    t_ss,
    t_rs,
):
    nctx = 2 * nz
    i = lax.axis_index("dp")
    c = lax.axis_index("ctx")
    z = lax.div(c, 2)
    k = lax.rem(c, 2)
    other = 1 - k
    seqs, width, span = cache.shape
    lat = wuk.shape[1]
    rope = width - lat
    heads = wuk.shape[0] // qn.shape[1]
    every = nctx * heads
    half = lat // 2

    def z_at(d):
        return lax.rem(z + d, nz)

    def z_peer(d):
        return (i, z_at(d) * 2 + k)

    partner = (i, z * 2 + other)

    def ctx_at(d):
        return lax.rem(c + d, nctx)

    def dp_at(d):
        return lax.rem(i + d, ndp)

    loads = [
        pltpu.make_async_copy(src, dst, load_sem.at[n])
        for n, (src, dst) in enumerate(
            (
                (wuk_hbm, wuk),
                (qn_hbm, qn),
                (qr_hbm, qr),
                (len_hbm, lengths),
                (wuv_hbm, wuv),
                (wout_hbm, wout),
            )
        )
    ]

    def cache_load(s):
        return pltpu.make_async_copy(cache_hbm.at[s], cache.at[s], cache_sem.at[s])

    loads[0].start()
    loads[1].start()

    barrier = pltpu.get_barrier_semaphore()

    def greet(peer):
        pl.semaphore_signal(barrier, inc=1, device_id=peer, device_id_type=MESH)

    for slot in range(nz - 1, 0, -1):
        greet(z_peer(AWAY[slot]))
    greet(partner)
    for d in range(1, ndp):
        greet((dp_at(d), c))

    loads[2].start()
    loads[3].start()
    loop(seqs, lambda s: cache_load(s).start())
    loads[4].start()
    loads[5].start()

    loads[2].wait()
    rows = qr[...].astype(F32)
    mid = seqs * heads // 2
    r_buf[k, 0] = jnp.concatenate([rows[:mid], rows[mid:]], axis=1).astype(BF16)

    loads[0].wait()
    loads[1].wait()
    q_lat = jnp.dot(spread(qn[...], heads), wuk[...], preferred_element_type=F32)
    for s in range(seqs):
        rows = q_lat[s * heads : (s + 1) * heads]
        q_buf[s, k, 0] = jnp.concatenate([rows[:, :half], rows[:, half:]], axis=0).astype(BF16)

    pl.semaphore_wait(barrier, nz + ndp - 1)

    def block_of(s, core, slot):
        return r_buf.at[core, slot] if isinstance(s, int) and s == seqs else q_buf.at[s, core, slot]

    def give(s, slot):
        return remote(
            block_of(s, k, 0),
            block_of(s, k, slot),
            q_ss.at[s, slot],
            q_rs.at[s, slot],
            z_peer(AWAY[slot]),
        )

    def hand(s, core):
        ref = r_buf.at[core] if isinstance(s, int) and s == seqs else q_buf.at[s, core]
        return remote(ref, ref, f_ss.at[s], f_rs.at[s], partner)

    order = (seqs,) + tuple(range(seqs))
    for s in order:
        for slot in range(nz - 1, 0, -1):
            give(s, slot).start()

    def pass_over(s):
        for slot in range(1, nz):
            give(s, slot).wait_recv()
        hand(s, k).start()

    def turn(s):
        cache_load(s).wait()
        for b in range(span // 256):
            part = cache[s, :lat, b * 256 : (b + 1) * 256]
            values[s, b * 256 : (b + 1) * 256, :] = part.T

    loop(seqs, turn)

    def st_copy(s):
        return remote(
            st_mine.at[s, other], st_other.at[s], p_ss.at[s, 0], p_rs.at[s, 0], partner
        )

    def acc_copy(s):
        return remote(
            acc_mine.at[s, other], acc_other.at[s], p_ss.at[s, 1], p_rs.at[s, 1], partner
        )

    def o_copy(s, slot):
        return remote(
            o_send.at[s, slot],
            o_recv.at[s, slot],
            o_ss.at[s, slot],
            o_rs.at[s, slot],
            z_peer((nz - AWAY[slot]) % nz),
        )

    def zs_copy(slot):
        return remote(
            zs_send.at[slot],
            zs_recv.at[slot],
            s_ss.at[slot],
            s_rs.at[slot],
            z_peer((nz - AWAY[slot]) % nz),
        )

    block = min(512, span)
    blocks = span // block

    def attend(s):
        for e in range(2):
            rows = q_buf[s, :, :, e * heads : (e + 1) * heads, :].astype(F32)
            qfull[:, e * half : (e + 1) * half] = rows.reshape(every, half).astype(BF16)
        ropes = r_buf[...].astype(F32).reshape(nctx, 2, heads, 2 * rope)
        odd = lax.rem(s, 2) == 1
        ropes = jnp.where(odd, ropes[:, 1], ropes[:, 0]).reshape(every, 2 * rope)
        late = s >= seqs // 2
        qfull[:, lat:] = jnp.where(late, ropes[:, rope:], ropes[:, :rope]).astype(BF16)
        top = jnp.full((every, 128), -1e30, F32)
        live = lengths[s] - c * span
        for b in range(blocks):
            part = jnp.dot(
                qfull[...],
                cache[s, :, b * block : (b + 1) * block],
                preferred_element_type=F32,
            )
            position = b * block + lax.broadcasted_iota(jnp.int32, part.shape, 1)
            part = jnp.where(position < live, part, -1e30)
            scores[:, b * block : (b + 1) * block] = part
            for e in range(block // 128):
                top = jnp.maximum(top, part[:, e * 128 : (e + 1) * 128])
        m2 = jnp.maximum(jnp.max(top, axis=1, keepdims=True) * scale2, FLOOR)
        total = jnp.zeros((every, 128), F32)
        for b in range(blocks):
            part = jnp.exp2(scores[:, b * block : (b + 1) * block] * scale2 - m2)
            probs[:, b * block : (b + 1) * block] = part.astype(BF16)
            for e in range(block // 128):
                total = total + part[:, e * 128 : (e + 1) * 128]
        l = jnp.sum(total, axis=1, keepdims=True)
        table = columns((every, 128), ((0, m2), (1, l)))
        st_mine[s, 0] = table[: every // 2]
        st_mine[s, 1] = table[every // 2 :]
        st_copy(s).start()
        acc = jnp.dot(probs[...], values[s], preferred_element_type=F32).astype(BF16)
        acc_mine[s, 0] = acc[: every // 2]
        acc_mine[s, 1] = acc[every // 2 :]
        acc_copy(s).start()

    def combine(s, last):
        st_copy(s).wait_recv()
        mine, theirs = st_mine[s, k], st_other[s]
        m_a, l_a = mine[:, 0:1], mine[:, 1:2]
        m_b, l_b = theirs[:, 0:1], theirs[:, 1:2]
        m = jnp.maximum(m_a, m_b)
        w_a, w_b = jnp.exp2(m_a - m), jnp.exp2(m_b - m)
        l = w_a * l_a + w_b * l_b
        table = columns((nz * heads, 128), ((2 * s, m), (2 * s + 1, l))).reshape(nz, heads, 128)
        if last:
            zs_send[...] += table

            for slot in range(nz - 1, 0, -1):
                zs_copy(slot).start()
            zs_recv[0] = zs_send[0]
        else:
            zs_send[...] += table
        acc_copy(s).wait_recv()
        joined = w_a * acc_mine[s, k].astype(F32) + w_b * acc_other[s].astype(F32)
        joined = joined.reshape(nz, heads, lat)
        joined = jnp.concatenate([joined[:, :, :half], joined[:, :, half:]], axis=1)
        o_send[s] = joined.astype(BF16)

        for slot in range(nz - 1, 0, -1):
            o_copy(s, slot).start()
        o_recv[s, 0] = o_send[s, 0]

    zs_send[...] = jnp.zeros_like(zs_send)
    pass_over(seqs)
    pass_over(0)
    hand(seqs, other).wait_recv()
    loads[3].wait()

    def step(s):
        @pl.when(s + 1 < seqs)
        def _():
            pass_over(s + 1)

        hand(s, other).wait_recv()
        attend(s)

        @pl.when(s > 0)
        def _():
            combine(s - 1, False)

    loop(seqs, step)
    combine(seqs - 1, True)

    def h_copy(p, d, slot):
        ref = heads_buf.at[p, slot]
        return remote(ref, ref, h_ss.at[p, d], h_rs.at[p, d], (dp_at(d), c))

    loads[4].wait()

    for slot in range(1, nz):
        zs_copy(slot).wait_recv()

    def finish(s, row):
        for slot in range(1, nz):
            o_copy(s, slot).wait_recv()
        lane = lax.broadcasted_iota(jnp.int32, (nz, heads, 128), 2)
        table = zs_recv[...]
        m = jnp.sum(jnp.where(lane == 2 * s, table, 0.0), axis=2, keepdims=True)
        l = jnp.sum(jnp.where(lane == 2 * s + 1, table, 0.0), axis=2, keepdims=True)
        top = jnp.max(m, axis=0, keepdims=True)
        w = jnp.exp2(m - top)
        w = w / jnp.sum(w * l, axis=0, keepdims=True)
        data = o_recv[s].astype(F32)
        left = jnp.sum(w * data[:, :heads], axis=0)
        right = jnp.sum(w * data[:, heads:], axis=0)
        latents[pl.ds(row, heads), :] = jnp.concatenate([left, right], axis=1)

    def project(p):
        for e in range(seqs // 2):
            finish(p * (seqs // 2) + e, e * heads)
        head_out = jnp.dot(
            spread(latents[...].astype(BF16), heads), wuv[...], preferred_element_type=F32
        )
        heads_buf[p, i] = head_out.astype(BF16)

        def give(n):
            h_copy(p, far_first(n, ndp), i).start()

        loop(ndp - 1, give)

    loop(2, project)
    loads[5].wait()

    def heads_arrive(n):
        p = lax.div(n, ndp - 1)
        d = near_first(lax.rem(n, ndp - 1), ndp)
        h_copy(p, d, dp_at(ndp - d)).wait_recv()

    loop(2 * (ndp - 1), heads_arrive)
    heads_f32[...] = heads_buf[...].astype(F32).reshape(heads_f32.shape)
    rows = ndp * seqs
    merged = jnp.concatenate(
        [heads_f32[pl.ds(h, rows, stride=heads), :] for h in range(heads)], axis=1
    ).astype(BF16)
    terms = dot_nt(merged, wout[...])
    cols = terms.shape[1]
    pieces = -(-cols // 128)
    for p in range(2):
        for n in range(pieces):
            piece = terms[p * rows // 2 : (p + 1) * rows // 2, n * 128 : min(cols, (n + 1) * 128)]
            if piece.shape[1] < 128:
                piece = jnp.concatenate(
                    [piece, jnp.zeros((rows // 2, 128 - piece.shape[1]), F32)], axis=1
                )
            sums_f32[pl.ds(p * pieces + n, rows // 2, stride=2 * pieces), :] = piece
    sums_send[...] = sums_f32[...].astype(BF16).reshape(sums_send.shape)

    def t_copy(d, at, slot):
        return remote(
            sums_send.at[at], sums_recv.at[slot], t_ss.at[d], t_rs.at[d], (i, ctx_at(d))
        )

    def t_start(n):
        d = far_first(n, nctx)
        t_copy(d, ctx_at(d), c).start()

    loop(nctx - 1, t_start)
    sums_recv[c] = sums_send[c]

    for slot in range(1, nz):
        zs_copy(slot).wait_send()
        give(seqs, slot).wait_send()
    hand(seqs, k).wait_send()

    def sent(s):
        hand(s, k).wait_send()
        for slot in range(1, nz):
            give(s, slot).wait_send()
        st_copy(s).wait_send()
        acc_copy(s).wait_send()
        for slot in range(1, nz):
            o_copy(s, slot).wait_send()

    loop(seqs, sent)

    def sent_heads(n):
        h_copy(0, n + 1, i).wait_send()
        h_copy(1, n + 1, i).wait_send()

    loop(ndp - 1, sent_heads)

    def sums_arrive(n):
        d = near_first(n, nctx)
        came = ctx_at(nctx - d)
        t_copy(d, came, came).wait_recv()

    loop(nctx - 1, sums_arrive)
    out_f32[...] = jnp.sum(sums_recv[...].astype(F32), axis=0)
    for p in range(2):
        for n in range(pieces):
            end = min(cols, (n + 1) * 128)
            piece = out_f32[pl.ds(p * pieces + n, seqs // 2, stride=2 * pieces), :]
            out_ref[p * seqs // 2 : (p + 1) * seqs // 2, n * 128 : end] = piece[
                :, : end - n * 128
            ].astype(BF16)

    loop(nctx - 1, lambda n: t_copy(n + 1, ctx_at(n + 1), c).wait_send())


def per_device(nz, ndp, q_nope, q_rope, w_uk, w_uv, w_out, latent_cache, lengths):
    seqs, heads, dn = q_nope.shape
    rope = q_rope.shape[2]
    lat = w_uk.shape[2]
    span = latent_cache.shape[1]
    dv = w_uv.shape[2]
    cols = w_out.shape[1]
    nctx = 2 * nz
    every = nctx * heads
    own = nz * heads
    pieces = -(-cols // 128)
    scale2 = math.log2(math.e) / math.sqrt(dn + rope)
    vmem, dma = pltpu.VMEM, pltpu.SemaphoreType.DMA
    hbm = pl.BlockSpec(memory_space=pltpu.HBM)
    return pl.pallas_call(
        functools.partial(kernel, nz, ndp, scale2),
        out_shape=jax.ShapeDtypeStruct((seqs, cols), BF16),
        in_specs=[hbm] * 7,
        out_specs=pl.BlockSpec(memory_space=vmem),
        scratch_shapes=[
            pltpu.SMEM((seqs,), jnp.int32),
            vmem((seqs * heads, dn), BF16),
            vmem((seqs * heads, rope), BF16),
            vmem((heads * dn, lat), BF16),
            vmem((heads * lat, dv), BF16),
            vmem((cols, heads * dv), BF16),
            vmem((seqs, lat + rope, span), BF16),
            vmem((seqs, span, lat), BF16),
            vmem((seqs, 2, nz, 2 * heads, lat // 2), BF16),
            vmem((2, nz, 2 * heads, 2 * rope), BF16),
            vmem((every, lat + rope), BF16),
            vmem((every, span), F32),
            vmem((every, span), BF16),
            vmem((seqs, 2, own, 128), F32),
            vmem((seqs, own, 128), F32),
            vmem((seqs, 2, own, lat), BF16),
            vmem((seqs, own, lat), BF16),
            vmem((nz, heads, 128), F32),
            vmem((nz, heads, 128), F32),
            vmem((seqs, nz, 2 * heads, lat // 2), BF16),
            vmem((seqs, nz, 2 * heads, lat // 2), BF16),
            vmem((seqs // 2 * heads, lat), F32),
            vmem((2, ndp, seqs // 2 * heads, dv), BF16),
            vmem((ndp * seqs * heads, dv), F32),
            vmem((ndp * seqs * pieces, 128), F32),
            vmem((nctx, seqs * pieces, 128), BF16),
            vmem((nctx, seqs * pieces, 128), BF16),
            vmem((seqs * pieces, 128), F32),
            dma((6,)),
            dma((seqs,)),
            dma((seqs + 1, nz)),
            dma((seqs + 1, nz)),
            dma((seqs + 1,)),
            dma((seqs + 1,)),
            dma((seqs, 2)),
            dma((seqs, 2)),
            dma((nz,)),
            dma((nz,)),
            dma((seqs, nz)),
            dma((seqs, nz)),
            dma((2, ndp)),
            dma((2, ndp)),
            dma((nctx,)),
            dma((nctx,)),
        ],
        compiler_params=pltpu.CompilerParams(
            collective_id=0, has_side_effects=True, vmem_limit_bytes=60 << 20
        ),
        name="mla_decode",
    )(
        lengths,
        q_nope.reshape(seqs * heads, dn),
        q_rope.reshape(seqs * heads, rope),
        w_uk.reshape(heads * dn, lat),
        w_uv.reshape(heads * lat, dv),
        w_out.T,
        jnp.swapaxes(latent_cache, 1, 2),
    )


def solution(mesh):
    in_specs = (
        P("dp", "ctx", None),
        P("dp", "ctx", None),
        P("ctx", None, None),
        P("ctx", None, None),
        P("ctx", "dp"),
        P("dp", "ctx", None),
        P("dp"),
    )
    out_specs = P("ctx", "dp")
    return jax.shard_map(
        functools.partial(per_device, mesh.shape["ctx"] // 2, mesh.shape["dp"]),
        mesh=mesh,
        in_specs=in_specs,
        out_specs=out_specs,
        check_vma=False,
    )
```

time: 47.3 us -> 45.6 us (0.964)
  Pallas kernels: 45.8 us -> 44.2 us
    pallas_call x1, Pallas kernels: 45.8 us -> 44.2 us  [per_device(): pl.pallas_call(functools.partial(kernel, nz, ndp, scale2), out_shape=jax....]
where the time goes in v2:
time: 45.6 us; the launch traced here: 45.5 us
  Pallas kernels  44.2 us (97%)
  local copies, waits for them, and re-layouts  1.28 us (3%)
    pallas_call x1, Pallas kernels, per_device(): pl.pallas_call(functools.partial(kernel, nz, ndp, scale2), out_shape=jax....  44.2 us
    unnamed x1, local copies, waits for them, and re-layouts  1.28 us

profile of v2, /device:TPU:1, one launch (start us, length us, event | category | flops | bytes accessed | tf_op | source)
XLA Modules:
  0.0 45.5 jit_solution(3378216452086392525)
XLA Ops:
  0.0 44.2 %mla_decode.1 = bf16[4,448]{1,0:T(4,128)(2,1)} custom-call(s32[4]{0:T(128)} %len_hbm.1, bf16[32,128]{1,0:T(8,128)(2,1)} %bitcast.10, bf16[32,64]{1,0:T(8,128)(2,1)} %bitcast.11, bf16[1024,512]{1,0:T(8,128)(2,1)} %bitcast.7, bf16[4096,128]{1,0:T(8,128)(2,1)} %bitcast.8, bf16[448,1024]{1,0:T(8,128)(2,1)} %bitcast.9, bf16[4,576,2048]{2,1,0:T(8,128)(2,1)} %bitcast.6), custom_call_target="tpu_custom_call" | custom-call | tf_op jit(solution)/shard_map/mla_decode/pallas_call | solution.py:476
  44.2 1.3 %copy.9 = bf16[4,448]{1,0:T(4,128)(2,1)} copy(bf16[4,448]{1,0:T(4,128)(2,1)} %mla_decode.1) | data formatting | bytes 7168

commit v3 on v2

--- a/solution.py
+++ b/solution.py
@@ -14,13 +14,12 @@
 FLOOR = -(2.0**90)
 
 
-def far_first(n, size):
-    step = lax.div(n + 1, 2)
-    return size // 2 + jnp.where(lax.rem(n, 2) == 1, -step, step)
-
-
-def near_first(n, size):
-    return far_first(size - 2 - n, size)
+def far_first(size):
+    return sorted(range(1, size), key=lambda d: -min(d, size - d))
+
+
+def near_first(size):
+    return sorted(range(1, size), key=lambda d: min(d, size - d))
 
 
 AWAY = (0, 1, 7, 2, 6, 3, 5, 4)
@@ -44,10 +43,6 @@
     row_head = lax.rem(lax.broadcasted_iota(jnp.int32, wide.shape, 0), heads)
     col_head = lax.div(lax.broadcasted_iota(jnp.int32, wide.shape, 1), width)
     return jnp.where(row_head == col_head, wide, 0.0).astype(BF16)
-
-
-def dot_nt(a, b):
-    return lax.dot_general(a, b, (((1,), (1,)), ((), ())), preferred_element_type=F32)
 
 
 def remote(src, dst, ss, rs, device):
@@ -74,6 +69,7 @@
     wuk,
     wuv,
     wout,
+    wout_t,
     cache,
     values,
     q_buf,
@@ -224,6 +220,8 @@
             values[s, b * 256 : (b + 1) * 256, :] = part.T
 
     loop(seqs, turn)
+    loads[5].wait()
+    wout_t[...] = wout[...].T
 
     def st_copy(s):
         return remote(
@@ -375,26 +373,20 @@
         )
         heads_buf[p, i] = head_out.astype(BF16)
 
-        def give(n):
-            h_copy(p, far_first(n, ndp), i).start()
-
-        loop(ndp - 1, give)
+        for d in far_first(ndp):
+            h_copy(p, d, i).start()
 
     loop(2, project)
-    loads[5].wait()
-
-    def heads_arrive(n):
-        p = lax.div(n, ndp - 1)
-        d = near_first(lax.rem(n, ndp - 1), ndp)
-        h_copy(p, d, dp_at(ndp - d)).wait_recv()
-
-    loop(2 * (ndp - 1), heads_arrive)
+
+    for p in range(2):
+        for d in near_first(ndp):
+            h_copy(p, d, dp_at(ndp - d)).wait_recv()
     heads_f32[...] = heads_buf[...].astype(F32).reshape(heads_f32.shape)
     rows = ndp * seqs
     merged = jnp.concatenate(
         [heads_f32[pl.ds(h, rows, stride=heads), :] for h in range(heads)], axis=1
     ).astype(BF16)
-    terms = dot_nt(merged, wout[...])
+    terms = jnp.dot(merged, wout_t[...], preferred_element_type=F32)
     cols = terms.shape[1]
     pieces = -(-cols // 128)
     for p in range(2):
@@ -412,11 +404,8 @@
             sums_send.at[at], sums_recv.at[slot], t_ss.at[d], t_rs.at[d], (i, ctx_at(d))
         )
 
-    def t_start(n):
-        d = far_first(n, nctx)
+    for d in far_first(nctx):
         t_copy(d, ctx_at(d), c).start()
-
-    loop(nctx - 1, t_start)
     sums_recv[c] = sums_send[c]
 
     for slot in range(1, nz):
@@ -441,12 +430,11 @@
 
     loop(ndp - 1, sent_heads)
 
-    def sums_arrive(n):
-        d = near_first(n, nctx)
+    for d in far_first(nctx):
+        t_copy(d, ctx_at(d), c).wait_send()
+    for d in near_first(nctx):
         came = ctx_at(nctx - d)
         t_copy(d, came, came).wait_recv()
-
-    loop(nctx - 1, sums_arrive)
     out_f32[...] = jnp.sum(sums_recv[...].astype(F32), axis=0)
     for p in range(2):
         for n in range(pieces):
@@ -455,8 +443,6 @@
             out_ref[p * seqs // 2 : (p + 1) * seqs // 2, n * 128 : end] = piece[
                 :, : end - n * 128
             ].astype(BF16)
-
-    loop(nctx - 1, lambda n: t_copy(n + 1, ctx_at(n + 1), c).wait_send())
 
 
 def per_device(nz, ndp, q_nope, q_rope, w_uk, w_uv, w_out, latent_cache, lengths):
@@ -485,6 +471,7 @@
             vmem((heads * dn, lat), BF16),
             vmem((heads * lat, dv), BF16),
             vmem((cols, heads * dv), BF16),
+            vmem((heads * dv, cols), BF16),
             vmem((seqs, lat + rope, span), BF16),
             vmem((seqs, span, lat), BF16),
             vmem((seqs, 2, nz, 2 * heads, lat // 2), BF16),

time: 45.6 us -> 45.1 us (0.989)
  Pallas kernels: 44.2 us -> 43.7 us
    pallas_call x1, Pallas kernels: 44.2 us -> 43.7 us  [per_device(): pl.pallas_call(functools.partial(kernel, nz, ndp, scale2), out_shape=jax....]
where the time goes in v3:
time: 45.1 us; the launch traced here: 45 us
  Pallas kernels  43.7 us (97%)
  local copies, waits for them, and re-layouts  1.28 us (3%)
    pallas_call x1, Pallas kernels, per_device(): pl.pallas_call(functools.partial(kernel, nz, ndp, scale2), out_shape=jax....  43.7 us
    unnamed x1, local copies, waits for them, and re-layouts  1.28 us

profile of v3, /device:TPU:1, one launch (start us, length us, event | category | flops | bytes accessed | tf_op | source)
XLA Modules:
  0.0 45.0 jit_solution(1502863589748602457)
XLA Ops:
  0.0 43.7 %mla_decode.1 = bf16[4,448]{1,0:T(4,128)(2,1)} custom-call(s32[4]{0:T(128)} %len_hbm.1, bf16[32,128]{1,0:T(8,128)(2,1)} %bitcast.10, bf16[32,64]{1,0:T(8,128)(2,1)} %bitcast.11, bf16[1024,512]{1,0:T(8,128)(2,1)} %bitcast.7, bf16[4096,128]{1,0:T(8,128)(2,1)} %bitcast.8, bf16[448,1024]{1,0:T(8,128)(2,1)} %bitcast.9, bf16[4,576,2048]{2,1,0:T(8,128)(2,1)} %bitcast.6), custom_call_target="tpu_custom_call" | custom-call | tf_op jit(solution)/shard_map/mla_decode/pallas_call | solution.py:462
  43.7 1.3 %copy.9 = bf16[4,448]{1,0:T(4,128)(2,1)} copy(bf16[4,448]{1,0:T(4,128)(2,1)} %mla_decode.1) | data formatting | bytes 7168

commit v4 on v3

--- a/solution.py
+++ b/solution.py
@@ -338,7 +338,8 @@
         def _():
             combine(s - 1, False)
 
-    loop(seqs, step)
+    for s in range(seqs):
+        step(s)
     combine(seqs - 1, True)
 
     def h_copy(p, d, slot):
@@ -376,7 +377,8 @@
         for d in far_first(ndp):
             h_copy(p, d, i).start()
 
-    loop(2, project)
+    for p in range(2):
+        project(p)
 
     for p in range(2):
         for d in near_first(ndp):

time: 45.1 us -> 44.8 us (level)
  no operation moved by 1% of the time
where the time goes in v4:
time: 44.8 us; the launch traced here: 44.7 us
  Pallas kernels  43.4 us (97%)
  local copies, waits for them, and re-layouts  1.28 us (3%)
    pallas_call x1, Pallas kernels, per_device(): pl.pallas_call(functools.partial(kernel, nz, ndp, scale2), out_shape=jax....  43.4 us
    unnamed x1, local copies, waits for them, and re-layouts  1.28 us

profile of v4, /device:TPU:1, one launch (start us, length us, event | category | flops | bytes accessed | tf_op | source)
XLA Modules:
  0.0 44.7 jit_solution(16763302675782101301)
XLA Ops:
  0.0 43.4 %mla_decode.1 = bf16[4,448]{1,0:T(4,128)(2,1)} custom-call(s32[4]{0:T(128)} %len_hbm.1, bf16[32,128]{1,0:T(8,128)(2,1)} %bitcast.10, bf16[32,64]{1,0:T(8,128)(2,1)} %bitcast.11, bf16[1024,512]{1,0:T(8,128)(2,1)} %bitcast.7, bf16[4096,128]{1,0:T(8,128)(2,1)} %bitcast.8, bf16[448,1024]{1,0:T(8,128)(2,1)} %bitcast.9, bf16[4,576,2048]{2,1,0:T(8,128)(2,1)} %bitcast.6), custom_call_target="tpu_custom_call" | custom-call | tf_op jit(solution)/shard_map/mla_decode/pallas_call | solution.py:464
  43.4 1.3 %copy.9 = bf16[4,448]{1,0:T(4,128)(2,1)} copy(bf16[4,448]{1,0:T(4,128)(2,1)} %mla_decode.1) | data formatting | bytes 7168

commit v5 on v4

--- a/solution.py
+++ b/solution.py
@@ -219,7 +219,8 @@
             part = cache[s, :lat, b * 256 : (b + 1) * 256]
             values[s, b * 256 : (b + 1) * 256, :] = part.T
 
-    loop(seqs, turn)
+    for s in range(seqs):
+        turn(s)
     loads[5].wait()
     wout_t[...] = wout[...].T
 
@@ -380,25 +381,24 @@
     for p in range(2):
         project(p)
 
+    rows = ndp * seqs // 2
+    cols = wout_t.shape[1]
+    pieces = -(-cols // 128)
     for p in range(2):
         for d in near_first(ndp):
             h_copy(p, d, dp_at(ndp - d)).wait_recv()
-    heads_f32[...] = heads_buf[...].astype(F32).reshape(heads_f32.shape)
-    rows = ndp * seqs
-    merged = jnp.concatenate(
-        [heads_f32[pl.ds(h, rows, stride=heads), :] for h in range(heads)], axis=1
-    ).astype(BF16)
-    terms = jnp.dot(merged, wout_t[...], preferred_element_type=F32)
-    cols = terms.shape[1]
-    pieces = -(-cols // 128)
-    for p in range(2):
+        heads_f32[p] = heads_buf[p].astype(F32).reshape(heads_f32.shape[1:])
+        merged = jnp.concatenate(
+            [heads_f32[p, pl.ds(h, rows, stride=heads), :] for h in range(heads)], axis=1
+        ).astype(BF16)
+        terms = jnp.dot(merged, wout_t[...], preferred_element_type=F32)
         for n in range(pieces):
-            piece = terms[p * rows // 2 : (p + 1) * rows // 2, n * 128 : min(cols, (n + 1) * 128)]
+            piece = terms[:, n * 128 : min(cols, (n + 1) * 128)]
             if piece.shape[1] < 128:
                 piece = jnp.concatenate(
-                    [piece, jnp.zeros((rows // 2, 128 - piece.shape[1]), F32)], axis=1
+                    [piece, jnp.zeros((rows, 128 - piece.shape[1]), F32)], axis=1
                 )
-            sums_f32[pl.ds(p * pieces + n, rows // 2, stride=2 * pieces), :] = piece
+            sums_f32[pl.ds(p * pieces + n, rows, stride=2 * pieces), :] = piece
     sums_send[...] = sums_f32[...].astype(BF16).reshape(sums_send.shape)
 
     def t_copy(d, at, slot):
@@ -491,7 +491,7 @@
             vmem((seqs, nz, 2 * heads, lat // 2), BF16),
             vmem((seqs // 2 * heads, lat), F32),
             vmem((2, ndp, seqs // 2 * heads, dv), BF16),
-            vmem((ndp * seqs * heads, dv), F32),
+            vmem((2, ndp * seqs // 2 * heads, dv), F32),
             vmem((ndp * seqs * pieces, 128), F32),
             vmem((nctx, seqs * pieces, 128), BF16),
             vmem((nctx, seqs * pieces, 128), BF16),

time: 44.8 us -> 44.3 us (0.989)
  Pallas kernels: 43.4 us -> 42.9 us
    pallas_call x1, Pallas kernels: 43.4 us -> 42.9 us  [per_device(): pl.pallas_call(functools.partial(kernel, nz, ndp, scale2), out_shape=jax....]
where the time goes in v5:
time: 44.3 us; the launch traced here: 44.2 us
  Pallas kernels  42.9 us (97%)
  local copies, waits for them, and re-layouts  1.28 us (3%)
    pallas_call x1, Pallas kernels, per_device(): pl.pallas_call(functools.partial(kernel, nz, ndp, scale2), out_shape=jax....  42.9 us
    unnamed x1, local copies, waits for them, and re-layouts  1.28 us

profile of v5, /device:TPU:1, one launch (start us, length us, event | category | flops | bytes accessed | tf_op | source)
XLA Modules:
  0.0 44.2 jit_solution(4816604805600092632)
XLA Ops:
  0.0 42.9 %mla_decode.1 = bf16[4,448]{1,0:T(4,128)(2,1)} custom-call(s32[4]{0:T(128)} %len_hbm.1, bf16[32,128]{1,0:T(8,128)(2,1)} %bitcast.10, bf16[32,64]{1,0:T(8,128)(2,1)} %bitcast.11, bf16[1024,512]{1,0:T(8,128)(2,1)} %bitcast.7, bf16[4096,128]{1,0:T(8,128)(2,1)} %bitcast.8, bf16[448,1024]{1,0:T(8,128)(2,1)} %bitcast.9, bf16[4,576,2048]{2,1,0:T(8,128)(2,1)} %bitcast.6), custom_call_target="tpu_custom_call" | custom-call | tf_op jit(solution)/shard_map/mla_decode/pallas_call | solution.py:464
  42.9 1.3 %copy.9 = bf16[4,448]{1,0:T(4,128)(2,1)} copy(bf16[4,448]{1,0:T(4,128)(2,1)} %mla_decode.1) | data formatting | bytes 7168
